TPU v7x, 256 devices: a whole 4x4x8 slice. The times are simulated.
256 devices in a mesh: arow: 8 (over z_hi, core), bcol: 32 (over y, x, z_lo).
Axes of the slice: x: 4, y: 4, z: 8 (z_hi: 4, z_lo: 2; z = z_hi * 2 + z_lo), core: 2. Of those that a mesh axis runs over, the one named last changes fastest.
Arguments:
- correlation: bfloat16 [2, 12, 4096, 4096], P(None, None, 'arow', 'bcol'), may hold values from -6 to 6
- freq_bins: int32 [12], replicated, may hold values from 1 to 1023
- coords_a: int32 [2, 4096], replicated, may hold values from 0 to 19999
- coords_b: int32 [2, 4096], replicated, may hold values from 0 to 19999
- assign_a: int32 [4096], P('arow'), may hold values from 0 to 4095, each once
- assign_b: int32 [4096], P('bcol'), may hold values from 0 to 4095, each once
- slow_a: int32 [2, 512], replicated, may hold values from -24 to 24
- slow_b: int32 [2, 512], replicated, may hold values from -24 to 24
Outputs:
- power: float32 [12, 512, 512], P(None, 'bcol', 'arow')
All inputs are finite; a program needn't handle non-finite values.
Results may differ from a plain program's by a relative error of at most 0.0034.
Values sent between devices are 32-bit elements; how exact they have to be, the bound alone decides.
A program may use at most 128 MiB of HBM per device.

v0:
```python
import math

import jax
import jax.numpy as jnp
from jax import lax
from jax.sharding import PartitionSpec as P

NA = 4096
NB = 4096


phase_modulus = 51200000


def steer(coords, assign, slow, freq, scale):
    place = jnp.take(coords, assign, axis=1)
    products = slow[0][:, None] * place[0][None, :] + slow[1][:, None] * place[1][None, :]
    turns = jnp.remainder(freq * products, phase_modulus)
    phase = turns.astype(jnp.float32) * jnp.float32(2.0 * math.pi / phase_modulus)
    real_part = (jnp.cos(phase) * scale).astype(jnp.bfloat16)
    imag_part = (-jnp.sin(phase) * scale).astype(jnp.bfloat16)
    return (real_part, imag_part)


def lowdot(form, left, right):
    return jnp.einsum(form, left, right, preferred_element_type=jnp.float32)


def highdot(form, left, right):
    return jnp.einsum(form, left, right, precision=lax.Precision.HIGHEST)


def body(correlation, freq_bins, coords_a, coords_b, assign_a, assign_b, slow_a, slow_b):
    bin_count = correlation.shape[1]
    bin_ids = jnp.arange(bin_count, dtype=jnp.int32)

    def per_bin(index):
        corr_re = correlation[0, index]
        corr_im = correlation[1, index]
        ua_re, ua_im = steer(coords_a, assign_a, slow_a, freq_bins[index], NA ** (-0.5))
        w_re = lowdot("pa,ab->pb", ua_re, corr_re) + lowdot("pa,ab->pb", ua_im, corr_im)
        w_im = lowdot("pa,ab->pb", ua_re, corr_im) - lowdot("pa,ab->pb", ua_im, corr_re)
        return jnp.stack([w_re, w_im])

    stacked = lax.map(per_bin, bin_ids)
    partial_a = lax.psum_scatter(
        jnp.transpose(stacked, (2, 1, 0, 3)), "arow", scatter_dimension=0, tiled=True
    )

    def second_b(index):
        ub_re, ub_im = steer(coords_b, assign_b, slow_b, freq_bins[index], NB ** (-0.5))
        right_re = ub_re.astype(jnp.float32)
        right_im = ub_im.astype(jnp.float32)
        w_re = partial_a[:, 0, index]
        w_im = partial_a[:, 1, index]
        y_re = highdot("qb,pb->qp", right_re, w_re) - highdot("qb,pb->qp", right_im, w_im)
        y_im = highdot("qb,pb->qp", right_re, w_im) + highdot("qb,pb->qp", right_im, w_re)
        return jnp.stack([y_re, y_im])

    summed = lax.psum_scatter(lax.map(second_b, bin_ids), "bcol", scatter_dimension=2, tiled=True)
    return summed[:, 0] * summed[:, 0] + summed[:, 1] * summed[:, 1]


def solution(mesh):
    return jax.shard_map(
        body,
        mesh=mesh,
        in_specs=(P(None, None, "arow", "bcol"), P(), P(), P(), P("arow"), P("bcol"), P(), P()),
        out_specs=P(None, "bcol", "arow"),
        check_vma=False,
    )
```

profile of v0, /device:TPU:32, one launch (start us, length us, event | category | flops | bytes accessed | tf_op | source)
XLA Modules:
  0.0 976.4 jit_solution(14187986913346625150)
XLA Ops:
  9.8 525.4 %while.26 = (s32[]{:T(128)}, f32[12,2,512,128]{3,0,1,2:T(8,128)}, s32[12]{0:T(128)S(1)}, s32[12]{0:T(128)}, s32[2,512]{1,0:T(2,128)}, /*index=5*/s32[512]{0:T(51...) while((s32[]{:T(128)}, f32[12,2,512,128]{3,0,1,2:T(8,128)}, ...), condition=%wide.region_1.2_spmd, body=%wide.region_0.1_spmd.sunk | while | flops 283906048 | bytes 5305531 | solution.py:45
  20.7 5.9 fusion.99
  26.6 5.9 fusion.96
  32.4 5.9 fusion.97
  39.0 14.6 %dynamic_update_slice.19 = f32[12,2,512,128]{3,0,1,2:T(8,128)} dynamic-update-slice(f32[12,2,512,128]{3,0,1,2:T(8,128)} %get-tuple-element.487, f32[1,2,512,128]{3,0,1,2:T(1,128)S(1)} %copy.18, s32[]{:T(128)} %get-tuple-element.486, s32[]{:T(128)} %constant.169.clone.1..sunk, s32[]{:T(128)} %constant.169.clone.1..sunk, s32[]{:T(128)} %constant.169.clone.1..sunk) | dynamic-update-slice | bytes 1048580 | tf_op jit(solution)/shard_map/while/body/jit(dynamic_update_index_in_dim)/dynamic_update_slice | solution.py:45
  64.4 5.9 fusion.99
  70.3 5.9 fusion.96
  76.2 5.9 fusion.97
  82.8 14.6 %dynamic_update_slice.19 = f32[12,2,512,128]{3,0,1,2:T(8,128)} dynamic-update-slice(f32[12,2,512,128]{3,0,1,2:T(8,128)} %get-tuple-element.487, f32[1,2,512,128]{3,0,1,2:T(1,128)S(1)} %copy.18, s32[]{:T(128)} %get-tuple-element.486, s32[]{:T(128)} %constant.169.clone.1..sunk, s32[]{:T(128)} %constant.169.clone.1..sunk, s32[]{:T(128)} %constant.169.clone.1..sunk) | dynamic-update-slice | bytes 1048580 | tf_op jit(solution)/shard_map/while/body/jit(dynamic_update_index_in_dim)/dynamic_update_slice | solution.py:45
  108.2 5.9 fusion.99
  114.1 5.9 fusion.96
  120.0 5.9 fusion.97
  126.5 14.6 %dynamic_update_slice.19 = f32[12,2,512,128]{3,0,1,2:T(8,128)} dynamic-update-slice(f32[12,2,512,128]{3,0,1,2:T(8,128)} %get-tuple-element.487, f32[1,2,512,128]{3,0,1,2:T(1,128)S(1)} %copy.18, s32[]{:T(128)} %get-tuple-element.486, s32[]{:T(128)} %constant.169.clone.1..sunk, s32[]{:T(128)} %constant.169.clone.1..sunk, s32[]{:T(128)} %constant.169.clone.1..sunk) | dynamic-update-slice | bytes 1048580 | tf_op jit(solution)/shard_map/while/body/jit(dynamic_update_index_in_dim)/dynamic_update_slice | solution.py:45
  152.0 5.9 fusion.99
  157.9 5.9 fusion.96
  163.7 5.9 fusion.97
  170.3 14.6 %dynamic_update_slice.19 = f32[12,2,512,128]{3,0,1,2:T(8,128)} dynamic-update-slice(f32[12,2,512,128]{3,0,1,2:T(8,128)} %get-tuple-element.487, f32[1,2,512,128]{3,0,1,2:T(1,128)S(1)} %copy.18, s32[]{:T(128)} %get-tuple-element.486, s32[]{:T(128)} %constant.169.clone.1..sunk, s32[]{:T(128)} %constant.169.clone.1..sunk, s32[]{:T(128)} %constant.169.clone.1..sunk) | dynamic-update-slice | bytes 1048580 | tf_op jit(solution)/shard_map/while/body/jit(dynamic_update_index_in_dim)/dynamic_update_slice | solution.py:45
  195.7 5.9 fusion.99
  201.6 5.9 fusion.96
  207.5 5.9 fusion.97
  214.1 14.6 %dynamic_update_slice.19 = f32[12,2,512,128]{3,0,1,2:T(8,128)} dynamic-update-slice(f32[12,2,512,128]{3,0,1,2:T(8,128)} %get-tuple-element.487, f32[1,2,512,128]{3,0,1,2:T(1,128)S(1)} %copy.18, s32[]{:T(128)} %get-tuple-element.486, s32[]{:T(128)} %constant.169.clone.1..sunk, s32[]{:T(128)} %constant.169.clone.1..sunk, s32[]{:T(128)} %constant.169.clone.1..sunk) | dynamic-update-slice | bytes 1048580 | tf_op jit(solution)/shard_map/while/body/jit(dynamic_update_index_in_dim)/dynamic_update_slice | solution.py:45
  239.5 5.9 fusion.99
  245.4 5.9 fusion.96
  251.3 5.9 fusion.97
  257.8 14.6 %dynamic_update_slice.19 = f32[12,2,512,128]{3,0,1,2:T(8,128)} dynamic-update-slice(f32[12,2,512,128]{3,0,1,2:T(8,128)} %get-tuple-element.487, f32[1,2,512,128]{3,0,1,2:T(1,128)S(1)} %copy.18, s32[]{:T(128)} %get-tuple-element.486, s32[]{:T(128)} %constant.169.clone.1..sunk, s32[]{:T(128)} %constant.169.clone.1..sunk, s32[]{:T(128)} %constant.169.clone.1..sunk) | dynamic-update-slice | bytes 1048580 | tf_op jit(solution)/shard_map/while/body/jit(dynamic_update_index_in_dim)/dynamic_update_slice | solution.py:45
  283.3 5.9 fusion.99
  289.2 5.9 fusion.96
  295.0 5.9 fusion.97
  301.6 14.6 %dynamic_update_slice.19 = f32[12,2,512,128]{3,0,1,2:T(8,128)} dynamic-update-slice(f32[12,2,512,128]{3,0,1,2:T(8,128)} %get-tuple-element.487, f32[1,2,512,128]{3,0,1,2:T(1,128)S(1)} %copy.18, s32[]{:T(128)} %get-tuple-element.486, s32[]{:T(128)} %constant.169.clone.1..sunk, s32[]{:T(128)} %constant.169.clone.1..sunk, s32[]{:T(128)} %constant.169.clone.1..sunk) | dynamic-update-slice | bytes 1048580 | tf_op jit(solution)/shard_map/while/body/jit(dynamic_update_index_in_dim)/dynamic_update_slice | solution.py:45
  327.0 5.9 fusion.99
  332.9 5.9 fusion.96
  338.8 5.9 fusion.97
  345.3 14.6 %dynamic_update_slice.19 = f32[12,2,512,128]{3,0,1,2:T(8,128)} dynamic-update-slice(f32[12,2,512,128]{3,0,1,2:T(8,128)} %get-tuple-element.487, f32[1,2,512,128]{3,0,1,2:T(1,128)S(1)} %copy.18, s32[]{:T(128)} %get-tuple-element.486, s32[]{:T(128)} %constant.169.clone.1..sunk, s32[]{:T(128)} %constant.169.clone.1..sunk, s32[]{:T(128)} %constant.169.clone.1..sunk) | dynamic-update-slice | bytes 1048580 | tf_op jit(solution)/shard_map/while/body/jit(dynamic_update_index_in_dim)/dynamic_update_slice | solution.py:45
  370.8 5.9 fusion.99
  382.6 5.9 fusion.97
  389.1 14.6 %dynamic_update_slice.19 = f32[12,2,512,128]{3,0,1,2:T(8,128)} dynamic-update-slice(f32[12,2,512,128]{3,0,1,2:T(8,128)} %get-tuple-element.487, f32[1,2,512,128]{3,0,1,2:T(1,128)S(1)} %copy.18, s32[]{:T(128)} %get-tuple-element.486, s32[]{:T(128)} %constant.169.clone.1..sunk, s32[]{:T(128)} %constant.169.clone.1..sunk, s32[]{:T(128)} %constant.169.clone.1..sunk) | dynamic-update-slice | bytes 1048580 | tf_op jit(solution)/shard_map/while/body/jit(dynamic_update_index_in_dim)/dynamic_update_slice | solution.py:45
  414.6 5.9 fusion.99
  426.4 5.9 fusion.97
  432.9 14.6 %dynamic_update_slice.19 = f32[12,2,512,128]{3,0,1,2:T(8,128)} dynamic-update-slice(f32[12,2,512,128]{3,0,1,2:T(8,128)} %get-tuple-element.487, f32[1,2,512,128]{3,0,1,2:T(1,128)S(1)} %copy.18, s32[]{:T(128)} %get-tuple-element.486, s32[]{:T(128)} %constant.169.clone.1..sunk, s32[]{:T(128)} %constant.169.clone.1..sunk, s32[]{:T(128)} %constant.169.clone.1..sunk) | dynamic-update-slice | bytes 1048580 | tf_op jit(solution)/shard_map/while/body/jit(dynamic_update_index_in_dim)/dynamic_update_slice | solution.py:45
  458.4 5.9 fusion.99
  470.2 5.9 fusion.97
  476.7 14.6 %dynamic_update_slice.19 = f32[12,2,512,128]{3,0,1,2:T(8,128)} dynamic-update-slice(f32[12,2,512,128]{3,0,1,2:T(8,128)} %get-tuple-element.487, f32[1,2,512,128]{3,0,1,2:T(1,128)S(1)} %copy.18, s32[]{:T(128)} %get-tuple-element.486, s32[]{:T(128)} %constant.169.clone.1..sunk, s32[]{:T(128)} %constant.169.clone.1..sunk, s32[]{:T(128)} %constant.169.clone.1..sunk) | dynamic-update-slice | bytes 1048580 | tf_op jit(solution)/shard_map/while/body/jit(dynamic_update_index_in_dim)/dynamic_update_slice | solution.py:45
  502.2 5.9 fusion.99
  514.0 5.9 fusion.97
  520.5 14.6 %dynamic_update_slice.19 = f32[12,2,512,128]{3,0,1,2:T(8,128)} dynamic-update-slice(f32[12,2,512,128]{3,0,1,2:T(8,128)} %get-tuple-element.487, f32[1,2,512,128]{3,0,1,2:T(1,128)S(1)} %copy.18, s32[]{:T(128)} %get-tuple-element.486, s32[]{:T(128)} %constant.169.clone.1..sunk, s32[]{:T(128)} %constant.169.clone.1..sunk, s32[]{:T(128)} %constant.169.clone.1..sunk) | dynamic-update-slice | bytes 1048580 | tf_op jit(solution)/shard_map/while/body/jit(dynamic_update_index_in_dim)/dynamic_update_slice | solution.py:45
  540.3 93.4 %reduce-scatter.3.cloned.1.call-done = f32[64,2,12,128]{3,2,1,0:T(8,128)} async-done(((f32[512,2,12,128]{3,2,1,0:T(8,128)}), f32[64,2,12,128]{3,2,1,0:T(8,128)}) %reduce-scatter.3.cloned.1.call-update) | async-done | bytes 786448 | tf_op jit(solution)/shard_map/reduce_scatter | solution.py:46
  633.7 147.5 %while.27 = (s32[]{:T(128)}, f32[12,2,512,64]{2,3,1,0:T(8,128)S(1)}, s32[12]{0:T(128)S(1)}, s32[12]{0:T(128)S(1)}, s32[2,512]{1,0:T(2,128)S(1)}, /*index=5*/s32[...) while((s32[]{:T(128)}, ...), condition=%wide.region_4.5_spmd, body=%wide.region_3.4_spmd.sunk | while | flops 205259776 | bytes 1606591 | solution.py:60
  785.3 182.6 %reduce-scatter.5.cloned.1.call-done = f32[12,2,16,64]{3,2,0,1:T(8,128)} async-done(((f32[12,2,512,64]{3,2,0,1:T(8,128)}), f32[12,2,16,64]{3,2,0,1:T(8,128)}) %reduce-scatter.5.cloned.1.call-update) | async-done | bytes 98320 | tf_op jit(solution)/shard_map/reduce_scatter | solution.py:60
  (284 shorter events, 278.5 us)
Async XLA Ops:
  6.5 627.1 %reduce-scatter.3.cloned.1.call-start = ((), (), s32[]{:S(2)}) async-start(), calls=%async_computation.2 | async-start | bytes 9437184 | tf_op jit(solution)/shard_map/reduce_scatter | solution.py:46
  535.2 0.8 copy-start.1
  535.2 2.8 copy-start.3
  535.2 98.5 %copy-start = (s32[2,512]{1,0:T(2,128)S(1)}, s32[2,512]{1,0:T(2,128)}, u32[]{:S(2)}) copy-start(s32[2,512]{1,0:T(2,128)} %param.19) | copy-start | bytes 12292
  535.2 98.5 %copy-start.2 = (s32[12]{0:T(128)S(1)}, s32[12]{0:T(128)}, u32[]{:S(2)}) copy-start(s32[12]{0:T(128)} %get-tuple-element.549) | copy-start | bytes 148
  535.2 432.7 %reduce-scatter.5.cloned.1.call-start = ((), (), s32[]{:S(2)}) async-start(), calls=%async_computation.3 | async-start | bytes 6488064 | tf_op jit(solution)/shard_map/reduce_scatter | solution.py:60
Sparse Core Ops, SparseCore 0:
  535.3 98.3 reduce-scatter.2
  785.4 182.4 reduce-scatter.4
where the time goes:
time: 987 us; the launch traced here: 976 us
  matrix products  377 us (38%)
  waiting for transfers between devices  276 us (28%)
  local copies, waits for them, and re-layouts  253 us (26%)
  loops' own time  44.3 us (4%)
  between operations  13.5 us (1%)
  other arithmetic  11.9 us (1%)
    dot_general x48, matrix products, lowdot(): return jnp.einsum(form, left, right, preferred_element_type=jnp.float32)  283 us
    reduce_scatter x1, waiting for transfers between devices, body(): lax.psum_scatter(lax.map(second_b, bin_ids), 'bcol', scatter_dimension=2,...  183 us
    dynamic_update_slice x24, local copies, waits for them, and re-layouts, body(): stacked = lax.map(per_bin, bin_ids)  182 us
    dot_general x48, matrix products, highdot(): return jnp.einsum(form, left, right, precision=lax.Precision.HIGHEST)  94.9 us
    reduce_scatter x1, waiting for transfers between devices, body(): lax.psum_scatter(jnp.transpose(stacked, (2, 1, 0, 3)), 'arow', scatter_di...  93.4 us
    another operation x1, loops' own time, body(): lax.map(second_b, bin_ids)  23.5 us
    another operation x1, loops' own time, body(): stacked = lax.map(per_bin, bin_ids)  20.9 us
  transfers between devices with their start and end apart: 2, of which 2 were waited for; matrix products, arithmetic and copies ran while one was open for 0% of the time, Pallas kernels for 0%

commit v1 on v0

v1 whole, which is shorter than its diff:
```python
import jax
import jax.numpy as jnp
from jax import lax
from jax.experimental import pallas as pl
from jax.experimental.pallas import tpu as pltpu
from jax.sharding import PartitionSpec as P

F = 12
ROUNDS = 3
LINE = 4
NZ = 8
MESH = pl.DeviceIdType.MESH

SIN = (4.442882834149931, -7.308241154546232, 3.6062889582237627, -0.8457635961366404, 0.10920575361787692)
COS = (1.4142134965650095, -6.978850988238499, 5.7394611706724765, -1.883562987243115, 0.3106981916942927)


def cos_sin(turns):
    r = turns.astype(jnp.float32) * jnp.float32(2.0**-32)
    u = r * r
    s = jnp.float32(SIN[4])
    c = jnp.float32(COS[4])
    for i in (3, 2, 1, 0):
        s = s * u + jnp.float32(SIN[i])
        c = c * u + jnp.float32(COS[i])
    s = s * r
    return 1.0 - s * s, s * c


def kernel(corr_hbm, xa_ref, sa_ref, xb_ref, sb_ref, out_ref,
           corr_v, rhs, cs_a, part, core_in, summed, line_in, coord_in,
           cs_b, v_hi, v_lo, y_part, y_in, z_out, z_in, f_out, f_in,
           corr_sem, core_ss, core_rs, line_ss, line_rs, coord_ss, coord_rs,
           y_ss, y_rs, z_ss, z_rs, f_ss, f_rs):
    arow = lax.axis_index("arow")
    bcol = lax.axis_index("bcol")
    core = arow % 2
    z = (arow // 2) * 2 + bcol % 2
    y = bcol // 8
    x = (bcol // 2) % 4
    g = x * (1 - core) + y * core
    h = y * (1 - core) + x * core

    def at(gg, hh, zz, cc_same=True):
        xx = gg * (1 - core) + hh * core
        yy = hh * (1 - core) + gg * core
        return ((zz // 2) * 2 + core, (yy * 4 + xx) * 2 + zz % 2)

    sibling = ((z // 2) * 2 + 1 - core, bcol)
    line_peer = [at((g + 1 + k) % LINE, h, z) for k in range(3)]
    y_peer = [at(g, (h + 1 + k) % LINE, z) for k in range(3)]
    z_peer = [at(g, h, (z + 1 + k) % NZ) for k in range(7)]

    loads = []
    for r in range(ROUNDS):
        cp = pltpu.make_async_copy(
            corr_hbm.at[:, pl.ds(r * 4, 4)], corr_v.at[:, pl.ds(r * 4, 4)], corr_sem.at[r]
        )
        cp.start()
        loads.append(cp)

    barrier = pltpu.get_barrier_semaphore()
    peers = [sibling] + line_peer + y_peer + z_peer
    for p in peers:
        pl.semaphore_signal(barrier, inc=1, device_id=p, device_id_type=MESH)
    pl.semaphore_wait(barrier, len(peers))

    def remote(src, dst, ss, rs, dev):
        return pltpu.make_async_remote_copy(
            src_ref=src, dst_ref=dst, send_sem=ss, recv_sem=rs, device_id=dev, device_id_type=MESH
        )

    def coord_copy(k):
        return remote(xb_ref.at[(g + 1 + k) % LINE], coord_in.at[k], coord_ss.at[k], coord_rs.at[k], line_peer[k])

    for k in range(3):
        coord_copy(k).start()

    def core_copy(s):
        return remote(part.at[s], core_in.at[s], core_ss.at[s], core_rs.at[s], sibling)

    def line_copy(r, k):
        return remote(
            summed.at[r * 4 + k], line_in.at[r * 3 + k], line_ss.at[r * 3 + k], line_rs.at[r * 3 + k], line_peer[k]
        )

    def a_side(b, half, dst):
        xs = xa_ref[b, 0:1, :]
        ys = xa_ref[b, 1:2, :]

        def steer(i, carry):
            rows = pl.ds(pl.multiple_of(i * 16, 16), 16)
            s0 = sa_ref[half, 0, rows, :]
            s1 = sa_ref[half, 1, rows, :]
            s0 = jnp.concatenate([s0] * 4, axis=1)
            s1 = jnp.concatenate([s1] * 4, axis=1)
            c, s = cos_sin(s0 * xs + s1 * ys)
            cs_a[rows, 0:512] = c.astype(jnp.bfloat16)
            cs_a[rows, 512:1024] = s.astype(jnp.bfloat16)
            return carry

        lax.fori_loop(0, 16, steer, 0)
        cr = corr_v[0, b]
        ci = corr_v[1, b]
        rhs[0:512, 0:128] = cr
        rhs[0:512, 128:256] = ci
        rhs[512:1024, 0:128] = -ci
        rhs[512:1024, 128:256] = cr
        dst[...] = jnp.dot(cs_a[...], rhs[...], preferred_element_type=jnp.float32)

    def finish(s):
        core_copy(s).wait_recv()
        summed[s] = summed[s] + core_in[s]

    def a_step(s, carry):
        r4 = (s // 4) * 4
        k = s % 4
        a_side(r4 + (h + 1 + k) % LINE, 1 - core, part.at[s])
        core_copy(s).start()
        a_side(r4 + (g + 1 + k) % LINE, core, summed.at[s])

        @pl.when(s > 0)
        def _():
            finish(s - 1)

            @pl.when(k > 0)
            def _():
                slot = (s // 4) * 3 + k - 1
                remote(
                    summed.at[s - 1], line_in.at[slot], line_ss.at[slot], line_rs.at[slot],
                    at((g + k) % LINE, h, z),
                ).start()

        return carry

    def b_steer(r):
        rows = [coord_in.at[0], coord_in.at[1], coord_in.at[2], xb_ref.at[g]]
        xs = jnp.concatenate([q[2 * r : 2 * r + 1, :] for q in rows], axis=1)
        ys = jnp.concatenate([q[2 * r + 1 : 2 * r + 2, :] for q in rows], axis=1)

        def steer(i, carry):
            rows = pl.ds(pl.multiple_of(i * 16, 16), 16)
            s0 = sb_ref[0, rows, :]
            s1 = sb_ref[1, rows, :]
            s0 = jnp.concatenate([s0] * 4, axis=1)
            s1 = jnp.concatenate([s1] * 4, axis=1)
            c, s = cos_sin(s0 * xs + s1 * ys)
            c = c.astype(jnp.bfloat16)
            s = s.astype(jnp.bfloat16)
            for k in range(4):
                cs_b[rows, k * 256 : k * 256 + 128] = c[:, k * 128 : k * 128 + 128]
                cs_b[rows, k * 256 + 128 : k * 256 + 256] = s[:, k * 128 : k * 128 + 128]
            return carry

        lax.fori_loop(0, 32, steer, 0)

    def y_copy(r, k):
        return remote(
            y_part.at[r, (h + 1 + k) % LINE], y_in.at[r * 3 + k], y_ss.at[r * 3 + k], y_rs.at[r * 3 + k], y_peer[k]
        )

    def b_side(r):
        b_steer(r)
        for k in range(4):
            if k < 3:
                line_copy(r, k).wait_recv()
            w = line_in[r * 3 + k] if k < 3 else summed[r * 4 + 3]
            hi = w.astype(jnp.bfloat16)
            lo = (w - hi.astype(jnp.float32)).astype(jnp.bfloat16)
            for dst, val in ((v_hi, hi), (v_lo, lo)):
                dst[0:256, k * 256 : k * 256 + 256] = val
                dst[256:512, k * 256 : k * 256 + 128] = val[:, 128:256]
                dst[256:512, k * 256 + 128 : k * 256 + 256] = -val[:, 0:128]

        for k in range(4):
            block = (h + 1 + k) % LINE
            steer = cs_b[pl.ds(pl.multiple_of(block * 128, 128), 128), :]
            dims = (((1,), (1,)), ((), ()))
            y_part[r, block] = lax.dot_general(
                steer, v_hi[...], dims, preferred_element_type=jnp.float32
            ) + lax.dot_general(steer, v_lo[...], dims, preferred_element_type=jnp.float32)
            if k < 3:
                y_copy(r, k).start()

    def z_copy(r, k):
        return remote(
            z_out.at[r, (z + 1 + k) % NZ], z_in.at[r * 7 + k], z_ss.at[r * 7 + k], z_rs.at[r * 7 + k], z_peer[k]
        )

    def z_send(r):
        for k in range(3):
            y_copy(r, k).wait_recv()
        t = y_part[r, h] + y_in[r * 3] + y_in[r * 3 + 1] + y_in[r * 3 + 2]
        for zh in range(4):
            for zl in range(2):
                piece = t[zl * 64 : zl * 64 + 64]
                z_out[r, zh * 2 + zl] = jnp.concatenate(
                    [piece[:, zh * 64 : zh * 64 + 64], piece[:, 256 + zh * 64 : 256 + zh * 64 + 64]], axis=1
                )
        for k in range(7):
            z_copy(r, k).start()

    def f_copy(r, k):
        return remote(
            f_out.at[r, (g + 1 + k) % LINE], f_in.at[r * 3 + k], f_ss.at[r * 3 + k], f_rs.at[r * 3 + k], line_peer[k]
        )

    def power(r):
        for k in range(7):
            z_copy(r, k).wait_recv()
        t = z_out[r, z]
        for k in range(7):
            t = t + z_in[r * 7 + k]
        t = t * jnp.float32(2.0**-12)
        t = t * t
        t = t + pltpu.roll(t, 64, 1)
        for i in range(4):
            f_out[r, i] = t[i * 16 : i * 16 + 16]
        for k in range(3):
            f_copy(r, k).start()
        out_ref[r * 4 + g] = f_out[r, g][:, 0:64]

    loads[0].wait()
    lax.fori_loop(0, 4, a_step, 0)
    loads[1].wait()
    lax.fori_loop(4, 8, a_step, 0)
    for k in range(3):
        coord_copy(k).wait_recv()
    b_side(0)
    loads[2].wait()
    lax.fori_loop(8, 12, a_step, 0)
    finish(11)
    b_side(1)
    z_send(0)
    b_side(2)
    z_send(1)
    power(0)
    z_send(2)
    power(1)
    power(2)
    for r in range(ROUNDS):
        for k in range(3):
            f_copy(r, k).wait_recv()
            out_ref[r * 4 + (g + 3 - k) % LINE] = f_in[r * 3 + k][:, 0:64]

    def drain_core(s, carry):
        core_copy(s).wait_send()
        return carry

    lax.fori_loop(0, F, drain_core, 0)
    for k in range(3):
        coord_copy(k).wait_send()
    for r in range(ROUNDS):
        for k in range(3):
            line_copy(r, k).wait_send()
            y_copy(r, k).wait_send()
            f_copy(r, k).wait_send()
        for k in range(7):
            z_copy(r, k).wait_send()


def fractions(freq, coords, assign):
    place = jnp.take(coords, assign, axis=1)
    product = freq[:, None, None] * place[None]
    whole = product // 3125
    rest = product - whole * 3125
    return (whole << 18) + (rest << 18) // 3125


def body(correlation, freq_bins, coords_a, coords_b, assign_a, assign_b, slow_a, slow_b):
    core = lax.axis_index("arow") % 2
    xa = fractions(freq_bins, coords_a, assign_a)
    xb = fractions(freq_bins, coords_b, assign_b)
    xb = xb.reshape(ROUNDS, LINE, 2, 128).transpose(1, 0, 2, 3).reshape(LINE, ROUNDS * 2, 128)
    xb = jnp.pad(xb, ((0, 0), (0, 2), (0, 0)))
    sa = slow_a.reshape(2, 4, 2, 64).transpose(2, 0, 1, 3).reshape(2, 2, 256)
    sa = jnp.broadcast_to(sa[..., None], (2, 2, 256, 128))
    sb = slow_b.reshape(2, 4, 4, 2, 16)
    sb = jnp.where(core == 0, sb.transpose(0, 1, 3, 2, 4).reshape(2, 512), sb.transpose(0, 2, 3, 1, 4).reshape(2, 512))
    sb = jnp.broadcast_to(sb[..., None], (2, 512, 128))

    f32, bf16 = jnp.float32, jnp.bfloat16
    vmem = pl.BlockSpec(memory_space=pltpu.VMEM)
    dma = pltpu.SemaphoreType.DMA
    return pl.pallas_call(
        kernel,
        out_shape=jax.ShapeDtypeStruct((F, 16, 64), f32),
        in_specs=[pl.BlockSpec(memory_space=pl.ANY), vmem, vmem, vmem, vmem],
        out_specs=vmem,
        scratch_shapes=[
            pltpu.VMEM((2, F, 512, 128), bf16),
            pltpu.VMEM((1024, 256), bf16),
            pltpu.VMEM((256, 1024), bf16),
            pltpu.VMEM((F, 256, 256), f32),
            pltpu.VMEM((F, 256, 256), f32),
            pltpu.VMEM((F, 256, 256), f32),
            pltpu.VMEM((9, 256, 256), f32),
            pltpu.VMEM((3, 8, 128), jnp.int32),
            pltpu.VMEM((512, 1024), bf16),
            pltpu.VMEM((512, 1024), bf16),
            pltpu.VMEM((512, 1024), bf16),
            pltpu.VMEM((ROUNDS, LINE, 128, 512), f32),
            pltpu.VMEM((9, 128, 512), f32),
            pltpu.VMEM((ROUNDS, NZ, 64, 128), f32),
            pltpu.VMEM((21, 64, 128), f32),
            pltpu.VMEM((ROUNDS, LINE, 16, 128), f32),
            pltpu.VMEM((9, 16, 128), f32),
            dma((3,)),
            dma((F,)), dma((F,)),
            dma((9,)), dma((9,)),
            dma((3,)), dma((3,)),
            dma((9,)), dma((9,)),
            dma((21,)), dma((21,)),
            dma((9,)), dma((9,)),
        ],
        compiler_params=pltpu.CompilerParams(
            collective_id=0, has_side_effects=True, vmem_limit_bytes=56 * 2**20
        ),
        cost_estimate=pl.CostEstimate(flops=7 * 10**9, bytes_accessed=4 * 10**6, transcendentals=0),
    )(correlation, xa, sa, xb, sb)


def solution(mesh):
    return jax.shard_map(
        body,
        mesh=mesh,
        in_specs=(P(None, None, "arow", "bcol"), P(), P(), P(), P("arow"), P("bcol"), P(), P()),
        out_specs=P(None, "bcol", "arow"),
        check_vma=False,
    )
```

time: 987 us -> 82.3 us (0.08)
  matrix products: 377 us -> 0 us
  waiting for transfers between devices: 276 us -> 0 us
  local copies, waits for them, and re-layouts: 253 us -> 8.68 us
  Pallas kernels: 0 us -> 70.8 us
  loops' own time: 44.3 us -> 0 us
  between operations: 13.5 us -> 0.19 us
  other arithmetic: 11.9 us -> 1.43 us
    dot_general x96 -> x0, matrix products: 377 us -> none  [the longest x48 283 us: lowdot(): return jnp.einsum(form, left, right, preferred_element_type=jnp.float32)]
    reduce_scatter x2 -> x0, waiting for transfers between devices: 276 us -> none  [the longest x1 183 us: body(): lax.psum_scatter(lax.map(second_b, bin_ids), 'bcol', scatter_dimension=2,...]
    dynamic_update_slice x24 -> x0, local copies, waits for them, and re-layouts: 182 us -> none  [body(): stacked = lax.map(per_bin, bin_ids)]
    pallas_call x0 -> x1, Pallas kernels: none -> 70.8 us  [body(): pl.pallas_call(kernel, out_shape=jax.ShapeDtypeStruct((F, 16, 64), f32),...]
    dynamic_slice x60 -> x0, local copies, waits for them, and re-layouts: 50.5 us -> none  [the longest x12 14.9 us: per_bin(): freq_bins[index]]
    another operation x2 -> x0, loops' own time: 44.3 us -> none  [the longest x1 23.5 us: body(): lax.map(second_b, bin_ids)]
  transfers between devices with their start and end apart: 2 -> 0, of which waited for: 2 -> 0; matrix products, arithmetic and copies ran while one was open for 0% -> 0% of each run, Pallas kernels for 0% -> 0%
where the time goes in v1:
time: 82.3 us; the launch traced here: 81.1 us
  Pallas kernels  70.8 us (86%)
  local copies, waits for them, and re-layouts  8.68 us (11%)
  other arithmetic  1.43 us (2%)
    pallas_call x1, Pallas kernels, body(): pl.pallas_call(kernel, out_shape=jax.ShapeDtypeStruct((F, 16, 64), f32),...  70.8 us
    unnamed x15, local copies, waits for them, and re-layouts  3.64 us
    gather x2, local copies, waits for them, and re-layouts, fractions(): place = jnp.take(coords, assign, axis=1)  1.68 us

profile of v1, /device:TPU:32, one launch (start us, length us, event | category | flops | bytes accessed | tf_op | source)
XLA Modules:
  0.0 81.1 jit_solution(7544598778212341862)
XLA Ops:
  0.0 0.0 copy-start.1
  0.0 0.0 copy-start.4
  0.0 0.0 copy-start.2
  0.0 0.0 copy-start
  0.0 1.4 %copy.17 = s32[2,4096]{0,1:T(8,128)S(1)} copy(s32[2,4096]{1,0:T(2,128)} %param.10) | data formatting | bytes 65536 | tf_op args[2]
  1.5 0.0 copy-done.1
  1.5 0.0 copy-start.5
  1.5 0.0 copy-start.3
  1.5 1.0 %gather_fusion = s32[512,2]{1,0:T(8,128)S(1)} fusion(s32[2,4096]{0,1:T(8,128)S(1)} %copy.17, s32[1024]{0:T(1024)S(1)} %pad_clamp_fusion.1), kind=kCustom, calls=%fused_computation | custom fusion | bytes 10240 | tf_op jit(solution)/shard_map/jit(_take)/gather | solution.py:263
  2.6 0.1 select_bitcast_fusion
  2.7 0.1 copy.18
  2.8 0.0 copy-done.4
  2.8 1.0 %fusion.1.xa_ref = s32[12,2,512]{2,1,0:T(2,128)} fusion(s32[2,512]{1,0:T(2,128)S(1)} %copy.18, s32[12]{0:T(128)S(1)} %copy-done.4), kind=kLoop, calls=%fused_computation.11 | loop fusion | flops 270336 | bytes 53296 | tf_op jit(solution)/shard_map/add | solution.py:267
  3.9 0.0 copy-done.2
  3.9 0.1 reshape.72
  4.0 0.1 broadcast_in_dim.44
  4.1 1.0 %broadcast_in_dim.45.sa_ref = s32[2,2,256,128]{3,2,1,0:T(8,128)} broadcast(s32[2,2,256]{2,1,0:T(2,128)S(1)} %broadcast_in_dim.44), dimensions={0,1,2} | broadcast | bytes 528384 | tf_op jit(solution)/shard_map/broadcast_in_dim | solution.py:277
  5.0 0.0 copy-done
  5.0 0.6 copy.21
  5.7 0.0 copy-done.5
  5.7 0.6 gather_fusion.1
  6.4 0.1 select_bitcast_fusion.1
  6.5 0.1 copy.22
  6.6 0.1 mul.56
  6.7 0.1 copy.20
  6.8 0.1 fusion.2
  6.9 0.6 pad.4.xb_ref
  7.5 0.0 copy-done.3
  7.5 0.1 reshape.73
  7.7 0.1 select_n.81
  7.8 1.0 %broadcast_in_dim.49.sb_ref = s32[2,512,128]{2,1,0:T(8,128)} broadcast(s32[2,512]{1,0:T(2,128)S(1)} %select_n.81), dimensions={0,1} | broadcast | bytes 528384 | tf_op jit(solution)/shard_map/broadcast_in_dim | solution.py:280
  8.8 70.8 %shard_map.82 = f32[12,16,64]{2,1,0:T(8,128)} custom-call(bf16[2,12,512,128]{3,2,1,0:T(8,128)(2,1)} %corr_hbm.1, s32[12,2,512]{2,1,0:T(2,128)} %fusion.1.xa_ref, s32[2,2,256,128]{3,2,1,0:T(8,128)} %broadcast_in_dim.45.sa_ref, s32[4,8,128]{2,1,0:T(8,128)} %pad.4.xb_ref, s32[2,512,128]{2,1,0:T(8,128)} %broadcast_in_dim.49.sb_ref), custom_call_target="tpu_custom_call" | custom-call | flops 7000000000 | bytes 4000000 | tf_op jit(solution)/shard_map/pallas_call | solution.py:285
  79.6 1.5 %copy.27 = f32[12,16,64]{2,1,0:T(8,128)} copy(f32[12,16,64]{2,1,0:T(8,128)} %shard_map.82) | data formatting | bytes 98304
  (13 shorter events, 0.1 us)
Async XLA Ops:
  0.0 1.5 %copy-start.1 = (s32[512]{0:T(512)S(1)}, s32[512]{0:T(512)}, u32[]{:S(2)}) copy-start(s32[512]{0:T(512)} %param.12) | copy-start | bytes 6148
  0.0 2.8 %copy-start.4 = (s32[12]{0:T(128)S(1)}, s32[12]{0:T(128)}, u32[]{:S(2)}) copy-start(s32[12]{0:T(128)} %param.9) | copy-start | bytes 148
  0.0 3.9 %copy-start.2 = (s32[2,512]{1,0:T(2,128)S(1)}, s32[2,512]{1,0:T(2,128)}, u32[]{:S(2)}) copy-start(s32[2,512]{1,0:T(2,128)} %param.14) | copy-start | bytes 12292
  0.0 5.0 %copy-start = (s32[2,4096]{1,0:T(2,128)S(1)}, s32[2,4096]{1,0:T(2,128)}, u32[]{:S(2)}) copy-start(s32[2,4096]{1,0:T(2,128)} %param.11) | copy-start | bytes 98308
  1.5 4.2 %copy-start.5 = (s32[128]{0:T(128)S(1)}, s32[128]{0:T(128)}, u32[]{:S(2)}) copy-start(s32[128]{0:T(128)} %param.13) | copy-start | bytes 1540
  1.5 6.0 %copy-start.3 = (s32[2,512]{1,0:T(2,128)S(1)}, s32[2,512]{1,0:T(2,128)}, u32[]{:S(2)}) copy-start(s32[2,512]{1,0:T(2,128)} %param.15) | copy-start | bytes 12292

commit v2 on v1

v2 whole, which is shorter than its diff:
```python
import jax
import jax.numpy as jnp
from jax import lax
from jax.experimental import pallas as pl
from jax.experimental.pallas import tpu as pltpu
from jax.sharding import PartitionSpec as P

F = 12
ROUNDS = 3
UNITS = 6
LINE = 4
NZ = 8
MESH = pl.DeviceIdType.MESH

SIN = (4.442882834149931, -7.308241154546232, 3.6062889582237627, -0.8457635961366404, 0.10920575361787692)
COS = (1.4142134965650095, -6.978850988238499, 5.7394611706724765, -1.883562987243115, 0.3106981916942927)


def cos_sin(turns):
    r = turns.astype(jnp.float32) * jnp.float32(2.0**-32)
    u = r * r
    s = jnp.float32(SIN[4])
    c = jnp.float32(COS[4])
    for i in (3, 2, 1, 0):
        s = s * u + jnp.float32(SIN[i])
        c = c * u + jnp.float32(COS[i])
    s = s * r
    return 1.0 - s * s, s * c


def fraction(freq, place):
    product = freq * place
    return product * 83 + (product.astype(jnp.float32) * jnp.float32(0.88608)).astype(jnp.int32)


def places(coords_ref, assign, grid):
    for i in range(32):
        grid[2 * i : 2 * i + 2, :] = coords_ref[:, i * 128 : i * 128 + 128]
    table = grid[...]
    high = (table >> 8).astype(jnp.float32).astype(jnp.bfloat16)
    low = (table & 255).astype(jnp.float32).astype(jnp.bfloat16)
    n = assign.shape[1]
    lane = lax.broadcasted_iota(jnp.int32, (128, n), 0)
    pick = jnp.where(lane == (assign & 127), 1.0, 0.0).astype(jnp.bfloat16)
    value = 256.0 * jnp.dot(high, pick, preferred_element_type=jnp.float32) + jnp.dot(
        low, pick, preferred_element_type=jnp.float32
    )
    row = lax.broadcasted_iota(jnp.int32, (64, n), 0)
    value = jnp.where((row >> 1) == (assign >> 7), value, 0.0)
    px = jnp.sum(jnp.where((row & 1) == 0, value, 0.0), axis=0, keepdims=True)
    py = jnp.sum(jnp.where((row & 1) == 1, value, 0.0), axis=0, keepdims=True)
    return px.astype(jnp.int32), py.astype(jnp.int32)


def columns(slow_row):
    wide = jnp.broadcast_to(slow_row.astype(jnp.float32), (128, 128)).astype(jnp.bfloat16)
    i = lax.broadcasted_iota(jnp.int32, (128, 128), 0)
    j = lax.broadcasted_iota(jnp.int32, (128, 128), 1)
    eye = jnp.where(i == j, 1.0, 0.0).astype(jnp.bfloat16)
    out = lax.dot_general(eye, wide, (((1,), (1,)), ((), ())), preferred_element_type=jnp.float32)
    return out.astype(jnp.int32)


def kernel(corr_hbm, freq_ref, coords_a_ref, coords_b_ref, assign_a_ref, assign_b_ref, slow_a_ref, slow_b_ref, out_ref,
           corr_v, grid_a, grid_b, place_a, place_b, sa, sb, rhs, cs_a, part, core_in, line_in, coord_in,
           cs_b, v_hi, v_lo, y_part, y_in1, y_fwd, y_in2, z_out, z_in, f_out, f_in,
           corr_sem, core_ss, core_rs, line_ss, line_rs, coord_ss, coord_rs,
           y1_ss, y1_rs, y2_ss, y2_rs, z_ss, z_rs, f_ss, f_rs):
    arow = lax.axis_index("arow")
    bcol = lax.axis_index("bcol")
    core = arow % 2
    z = (arow // 2) * 2 + bcol % 2
    y = bcol // 8
    x = (bcol // 2) % 4
    g = x * (1 - core) + y * core
    h = y * (1 - core) + x * core

    def at(gg, hh, zz):
        xx = gg * (1 - core) + hh * core
        yy = hh * (1 - core) + gg * core
        return ((zz // 2) * 2 + core, (yy * 4 + xx) * 2 + zz % 2)

    near = h + 1 - 2 * (h % 2)
    wrap = 3 - h
    diagonal = 3 - near
    sibling = ((z // 2) * 2 + 1 - core, bcol)
    line_peer = [at((g + 1 + k) % LINE, h, z) for k in range(3)]
    z_peer = [at(g, h, (z + 1 + k) % NZ) for k in range(7)]

    loads = []
    for r in range(ROUNDS):
        cp = pltpu.make_async_copy(
            corr_hbm.at[:, pl.ds(r * 4, 4)], corr_v.at[:, pl.ds(r * 4, 4)], corr_sem.at[r]
        )
        cp.start()
        loads.append(cp)

    barrier = pltpu.get_barrier_semaphore()
    peers = [sibling, at(g, near, z), at(g, wrap, z)] + line_peer + z_peer
    for p in peers:
        pl.semaphore_signal(barrier, inc=1, device_id=p, device_id_type=MESH)

    bx, by = places(coords_b_ref, assign_b_ref[...], grid_b)
    place_b[...] = jnp.zeros_like(place_b)
    place_b[0:1, :] = bx
    place_b[1:2, :] = by
    ax, ay = places(coords_a_ref, assign_a_ref[...], grid_a)
    place_a[0:1, :] = ax
    place_a[1:2, :] = ay
    for i in range(2):
        for t in range(4):
            c = columns(slow_a_ref[i : i + 1, t * 128 : t * 128 + 128])
            sa[i, t * 64 : t * 64 + 64, :] = c[0:64]
            sa[i, 256 + t * 64 : 256 + t * 64 + 64, :] = c[64:128]
            c = columns(slow_b_ref[i : i + 1, t * 128 : t * 128 + 128])
            for xx in range(4):
                gg = xx * (1 - core) + t * core
                hh = t * (1 - core) + xx * core
                for zl in range(2):
                    for half in range(2):
                        src = (xx * 2 + zl) * 16 + half * 8
                        dst = pl.multiple_of(half * 256 + hh * 64 + zl * 32 + gg * 8, 8)
                        sb[i, pl.ds(dst, 8), :] = c[src : src + 8]

    pl.semaphore_wait(barrier, len(peers))

    def remote(src, dst, ss, rs, dev):
        return pltpu.make_async_remote_copy(
            src_ref=src, dst_ref=dst, send_sem=ss, recv_sem=rs, device_id=dev, device_id_type=MESH
        )

    def coord_copy(k):
        return remote(place_b, coord_in.at[k], coord_ss.at[k], coord_rs.at[k], line_peer[k])

    for k in range(3):
        coord_copy(k).start()

    def core_copy(s):
        return remote(part.at[s, 1 - core], core_in.at[s], core_ss.at[s], core_rs.at[s], sibling)

    def line_copy(s, slot, rel):
        return remote(
            part.at[s, core], line_in.at[slot], line_ss.at[slot], line_rs.at[slot], at((g + rel) % LINE, h, z)
        )

    def steer_rows(s_ref, xs, ys, put):
        def steer(i, carry):
            rows = pl.ds(pl.multiple_of(i * 16, 16), 16)
            s0 = s_ref[0, rows, :]
            s1 = s_ref[1, rows, :]
            s0 = jnp.concatenate([s0] * 4, axis=1)
            s1 = jnp.concatenate([s1] * 4, axis=1)
            c, s = cos_sin(s0 * xs + s1 * ys)
            put(rows, c.astype(jnp.bfloat16), s.astype(jnp.bfloat16))
            return carry

        lax.fori_loop(0, 32, steer, 0, unroll=4)

    def a_step(s, carry):
        k = s % 4
        b = (s // 4) * 4 + (x + y + 1 + k) % LINE
        freq = freq_ref[b]

        def put(rows, c, s_):
            cs_a[rows, 0:512] = c
            cs_a[rows, 512:1024] = s_

        steer_rows(sa, fraction(freq, place_a[0:1, :]), fraction(freq, place_a[1:2, :]), put)
        cr = corr_v[0, b]
        ci = corr_v[1, b]
        rhs[0:512, 0:128] = cr
        rhs[0:512, 128:256] = ci
        rhs[512:1024, 0:128] = -ci
        rhs[512:1024, 128:256] = cr
        w = jnp.dot(cs_a[...], rhs[...], preferred_element_type=jnp.float32)
        part[s, 0] = w[0:256]
        part[s, 1] = w[256:512]
        core_copy(s).start()

        @pl.when(s > 0)
        def _():
            finish(s - 1)

        return carry

    def finish(s):
        core_copy(s).wait_recv()
        part[s, core] = part[s, core] + core_in[s]
        rel = (h + 1 + s % 4) % LINE

        @pl.when(rel > 0)
        def _():
            line_copy(s, (s // 4) * 3 + rel - 1, rel).start()

    def b_steer(r):
        rows = [coord_in.at[0], coord_in.at[1], coord_in.at[2], place_b]
        freq = freq_ref[r * 4 + g]
        xs = fraction(freq, jnp.concatenate([q[0:1, :] for q in rows], axis=1))
        ys = fraction(freq, jnp.concatenate([q[1:2, :] for q in rows], axis=1))

        def put(rows, c, s):
            for k in range(4):
                cs_b[rows, k * 256 : k * 256 + 128] = c[:, k * 128 : k * 128 + 128]
                cs_b[rows, k * 256 + 128 : k * 256 + 256] = s[:, k * 128 : k * 128 + 128]

        steer_rows(sb, xs, ys, put)

    def pair(half):
        return (near, wrap) if half == 0 else (wrap, near)

    def y1_copy(u, j):
        first, _ = pair(u % 2)
        block = diagonal if j == 0 else first
        return remote(
            y_part.at[u, block], y_in1.at[u, j], y1_ss.at[u * 2 + j], y1_rs.at[u * 2 + j], at(g, first, z)
        )

    def y2_copy(u):
        _, second = pair(u % 2)
        return remote(y_fwd.at[u], y_in2.at[u], y2_ss.at[u], y2_rs.at[u], at(g, second, z))

    def b_side(r):
        b_steer(r)
        for k in range(4):
            if k < 3:
                line_copy(0, r * 3 + k, k + 1).wait_recv()
            w = line_in[r * 3 + k] if k < 3 else part[r * 4 + 3 - h, core]
            hi = w.astype(jnp.bfloat16)
            lo = (w - hi.astype(jnp.float32)).astype(jnp.bfloat16)
            for dst, val in ((v_hi, hi), (v_lo, lo)):
                dst[0:256, k * 256 : k * 256 + 256] = val
                dst[256:512, k * 256 : k * 256 + 128] = val[:, 128:256]
                dst[256:512, k * 256 + 128 : k * 256 + 256] = -val[:, 0:128]

        dims = (((1,), (1,)), ((), ()))
        for half in range(2):
            u = r * 2 + half
            steer = cs_b[half * 256 : half * 256 + 256, :]
            v = lax.dot_general(steer, v_hi[...], dims, preferred_element_type=jnp.float32)
            v = v + lax.dot_general(steer, v_lo[...], dims, preferred_element_type=jnp.float32)
            for i in range(4):
                y_part[u, i] = v[i * 64 : i * 64 + 64]
            for j in range(2):
                y1_copy(u, j).start()

    def y_forward(u):
        _, second = pair(u % 2)
        y1_copy(u, 0).wait_recv()
        y_fwd[u] = y_part[u, second] + y_in1[u, 0]
        y2_copy(u).start()

    def z_copy(u, k):
        return remote(
            z_out.at[u, (z + 1 + k) % NZ], z_in.at[u * 7 + k], z_ss.at[u * 7 + k], z_rs.at[u * 7 + k], z_peer[k]
        )

    def z_send(u):
        y1_copy(u, 1).wait_recv()
        y2_copy(u).wait_recv()
        t = y_part[u, h] + y_in1[u, 1] + y_in2[u]
        for zh in range(4):
            for zl in range(2):
                piece = t[zl * 32 : zl * 32 + 32]
                z_out[u, zh * 2 + zl] = jnp.concatenate(
                    [piece[:, zh * 64 : zh * 64 + 64], piece[:, 256 + zh * 64 : 256 + zh * 64 + 64]], axis=1
                )
        for k in (3, 2, 4, 1, 5, 0, 6):
            z_copy(u, k).start()

    def f_copy(u, k):
        return remote(
            f_out.at[u, (g + 1 + k) % LINE], f_in.at[u * 3 + k], f_ss.at[u * 3 + k], f_rs.at[u * 3 + k], line_peer[k]
        )

    def power(u):
        for k in range(7):
            z_copy(u, k).wait_recv()
        t = z_out[u, z]
        for k in range(7):
            t = t + z_in[u * 7 + k]
        t = t * jnp.float32(2.0**-12)
        t = t * t
        t = t + pltpu.roll(t, 64, 1)
        for i in range(4):
            f_out[u, i] = t[i * 8 : i * 8 + 8]
        for k in range(3):
            f_copy(u, k).start()
        out_ref[(u // 2) * 4 + g, (u % 2) * 8 : (u % 2) * 8 + 8, :] = f_out[u, g][:, 0:64]

    def each(fn, *units):
        for u in units:
            fn(u)

    loads[0].wait()
    lax.fori_loop(0, 4, a_step, 0)
    loads[1].wait()
    lax.fori_loop(4, 8, a_step, 0)
    for k in range(3):
        coord_copy(k).wait_recv()
    b_side(0)
    loads[2].wait()
    lax.fori_loop(8, 12, a_step, 0)
    finish(11)
    each(y_forward, 0, 1)
    b_side(1)
    each(z_send, 0, 1)
    each(y_forward, 2, 3)
    b_side(2)
    each(z_send, 2, 3)
    each(power, 0, 1)
    each(y_forward, 4, 5)
    each(power, 2, 3)
    each(z_send, 4, 5)
    each(power, 4, 5)
    for u in range(UNITS):
        for k in range(3):
            f_copy(u, k).wait_recv()
            out_ref[(u // 2) * 4 + (g + 3 - k) % LINE, (u % 2) * 8 : (u % 2) * 8 + 8, :] = f_in[u * 3 + k][:, 0:64]

    def drain_core(s, carry):
        core_copy(s).wait_send()
        return carry

    lax.fori_loop(0, F, drain_core, 0)
    for k in range(3):
        coord_copy(k).wait_send()
    for slot in range(9):
        line_copy(0, slot, slot % 3 + 1).wait_send()
    for u in range(UNITS):
        for j in range(2):
            y1_copy(u, j).wait_send()
        y2_copy(u).wait_send()
        for k in range(7):
            z_copy(u, k).wait_send()
        for k in range(3):
            f_copy(u, k).wait_send()


def body(correlation, freq_bins, coords_a, coords_b, assign_a, assign_b, slow_a, slow_b):
    i32, f32, bf16 = jnp.int32, jnp.float32, jnp.bfloat16
    vmem = pl.BlockSpec(memory_space=pltpu.VMEM)
    dma = pltpu.SemaphoreType.DMA
    return pl.pallas_call(
        kernel,
        out_shape=jax.ShapeDtypeStruct((F, 16, 64), f32),
        in_specs=[pl.BlockSpec(memory_space=pl.ANY), pl.BlockSpec(memory_space=pltpu.SMEM)] + [vmem] * 6,
        out_specs=vmem,
        scratch_shapes=[
            pltpu.VMEM((2, F, 512, 128), bf16),
            pltpu.VMEM((64, 128), i32),
            pltpu.VMEM((64, 128), i32),
            pltpu.VMEM((8, 512), i32),
            pltpu.VMEM((8, 128), i32),
            pltpu.VMEM((2, 512, 128), i32),
            pltpu.VMEM((2, 512, 128), i32),
            pltpu.VMEM((1024, 256), bf16),
            pltpu.VMEM((512, 1024), bf16),
            pltpu.VMEM((F, 2, 256, 256), f32),
            pltpu.VMEM((F, 256, 256), f32),
            pltpu.VMEM((9, 256, 256), f32),
            pltpu.VMEM((3, 8, 128), i32),
            pltpu.VMEM((512, 1024), bf16),
            pltpu.VMEM((512, 1024), bf16),
            pltpu.VMEM((512, 1024), bf16),
            pltpu.VMEM((UNITS, LINE, 64, 512), f32),
            pltpu.VMEM((UNITS, 2, 64, 512), f32),
            pltpu.VMEM((UNITS, 64, 512), f32),
            pltpu.VMEM((UNITS, 64, 512), f32),
            pltpu.VMEM((UNITS, NZ, 32, 128), f32),
            pltpu.VMEM((UNITS * 7, 32, 128), f32),
            pltpu.VMEM((UNITS, LINE, 8, 128), f32),
            pltpu.VMEM((UNITS * 3, 8, 128), f32),
            dma((3,)),
            dma((F,)), dma((F,)),
            dma((9,)), dma((9,)),
            dma((3,)), dma((3,)),
            dma((12,)), dma((12,)),
            dma((UNITS,)), dma((UNITS,)),
            dma((UNITS * 7,)), dma((UNITS * 7,)),
            dma((UNITS * 3,)), dma((UNITS * 3,)),
        ],
        compiler_params=pltpu.CompilerParams(
            collective_id=0, has_side_effects=True, vmem_limit_bytes=56 * 2**20
        ),
        cost_estimate=pl.CostEstimate(flops=7 * 10**9, bytes_accessed=4 * 10**6, transcendentals=0),
    )(correlation, freq_bins, coords_a, coords_b, assign_a.reshape(1, 512), assign_b.reshape(1, 128), slow_a, slow_b)


def solution(mesh):
    return jax.shard_map(
        body,
        mesh=mesh,
        in_specs=(P(None, None, "arow", "bcol"), P(), P(), P(), P("arow"), P("bcol"), P(), P()),
        out_specs=P(None, "bcol", "arow"),
        check_vma=False,
    )
```

time: 82.3 us -> 70.2 us (0.85)
  local copies, waits for them, and re-layouts: 8.68 us -> 1.54 us
  Pallas kernels: 70.8 us -> 67.8 us
  other arithmetic: 1.43 us -> 0 us
    pallas_call x1, Pallas kernels: 70.8 us -> 67.8 us  [body(): pl.pallas_call(kernel, out_shape=jax.ShapeDtypeStruct((F, 16, 64), f32),...]
    unnamed x15 -> x1, local copies, waits for them, and re-layouts: 3.64 us -> 1.54 us
    broadcast_in_dim x3 -> x0, local copies, waits for them, and re-layouts: 2.07 us -> none  [the longest x2 1.08 us: body(): sa = jnp.broadcast_to(sa[..., None], (2, 2, 256, 128))]
    gather x2 -> x0, local copies, waits for them, and re-layouts: 1.68 us -> none  [fractions(): place = jnp.take(coords, assign, axis=1)]
    add x2 -> x0, other arithmetic: 1.16 us -> none  [fractions(): return (whole << 18) + (rest << 18) // 3125]
where the time goes in v2:
time: 70.2 us; the launch traced here: 69.3 us
  Pallas kernels  67.8 us (97%)
  local copies, waits for them, and re-layouts  1.54 us (2%)
    pallas_call x1, Pallas kernels, body(): pl.pallas_call(kernel, out_shape=jax.ShapeDtypeStruct((F, 16, 64), f32),...  67.8 us
    unnamed x1, local copies, waits for them, and re-layouts  1.54 us

profile of v2, /device:TPU:32, one launch (start us, length us, event | category | flops | bytes accessed | tf_op | source)
XLA Modules:
  0.0 69.3 jit_solution(18348858430575526724)
XLA Ops:
  0.0 67.8 %shard_map.82 = f32[12,16,64]{2,1,0:T(8,128)} custom-call(bf16[2,12,512,128]{3,2,1,0:T(8,128)(2,1)} %corr_hbm.1, s32[12]{0:T(128)} %freq_ref.1, s32[2,4096]{1,0:T(2,128)} %coords_a_ref.1, s32[2,4096]{1,0:T(2,128)} %coords_b_ref.1, s32[1,512]{1,0:T(1,128)} %bitcast.2, s32[1,128]{1,0:T(1,128)} %bitcast.3, s32[2,512]{1,0:T(2,128)} %slow_a_ref.1, ...), custom_call_target="tpu_custom_call" | custom-call | flops 7000000000 | bytes 4000000 | tf_op jit(solution)/shard_map/pallas_call | solution.py:343
  67.8 1.5 %copy.10 = f32[12,16,64]{2,1,0:T(8,128)} copy(f32[12,16,64]{2,1,0:T(8,128)} %shard_map.82) | data formatting | bytes 98304

commit v3 on v2

--- a/solution.py
+++ b/solution.py
@@ -62,8 +62,8 @@
 
 
 def kernel(corr_hbm, freq_ref, coords_a_ref, coords_b_ref, assign_a_ref, assign_b_ref, slow_a_ref, slow_b_ref, out_ref,
-           corr_v, grid_a, grid_b, place_a, place_b, sa, sb, rhs, cs_a, part, core_in, line_in, coord_in,
-           cs_b, v_hi, v_lo, y_part, y_in1, y_fwd, y_in2, z_out, z_in, f_out, f_in,
+           corr_v, grid_a, grid_b, place_a, place_b, sa, sb, rhs, cs_0, cs_1, cs_2, cs_3, turns_0, turns_1, turns_2, turns_3, part, core_in, line_in, coord_in,
+           v_hi, v_lo, y_part, y_in1, y_fwd, y_in2, z_out, z_in, f_out, f_in,
            corr_sem, core_ss, core_rs, line_ss, line_rs, coord_ss, coord_rs,
            y1_ss, y1_rs, y2_ss, y2_rs, z_ss, z_rs, f_ss, f_rs):
     arow = lax.axis_index("arow")
@@ -87,13 +87,16 @@
     line_peer = [at((g + 1 + k) % LINE, h, z) for k in range(3)]
     z_peer = [at(g, h, (z + 1 + k) % NZ) for k in range(7)]
 
-    loads = []
+    def each(fn, *units):
+        for u in units:
+            fn(u)
+
+    def load(r):
+        four = pl.ds(r * 4, 4)
+        return pltpu.make_async_copy(corr_hbm.at[:, four], corr_v.at[:, four], corr_sem.at[r])
+
     for r in range(ROUNDS):
-        cp = pltpu.make_async_copy(
-            corr_hbm.at[:, pl.ds(r * 4, 4)], corr_v.at[:, pl.ds(r * 4, 4)], corr_sem.at[r]
-        )
-        cp.start()
-        loads.append(cp)
+        load(r).start()
 
     barrier = pltpu.get_barrier_semaphore()
     peers = [sibling, at(g, near, z), at(g, wrap, z)] + line_peer + z_peer
@@ -105,6 +108,7 @@
     place_b[0:1, :] = bx
     place_b[1:2, :] = by
     ax, ay = places(coords_a_ref, assign_a_ref[...], grid_a)
+    place_a[...] = jnp.zeros_like(place_a)
     place_a[0:1, :] = ax
     place_a[1:2, :] = ay
     for i in range(2):
@@ -122,8 +126,6 @@
                         dst = pl.multiple_of(half * 256 + hh * 64 + zl * 32 + gg * 8, 8)
                         sb[i, pl.ds(dst, 8), :] = c[src : src + 8]
 
-    pl.semaphore_wait(barrier, len(peers))
-
     def remote(src, dst, ss, rs, dev):
         return pltpu.make_async_remote_copy(
             src_ref=src, dst_ref=dst, send_sem=ss, recv_sem=rs, device_id=dev, device_id_type=MESH
@@ -132,9 +134,6 @@
     def coord_copy(k):
         return remote(place_b, coord_in.at[k], coord_ss.at[k], coord_rs.at[k], line_peer[k])
 
-    for k in range(3):
-        coord_copy(k).start()
-
     def core_copy(s):
         return remote(part.at[s, 1 - core], core_in.at[s], core_ss.at[s], core_rs.at[s], sibling)
 
@@ -143,45 +142,45 @@
             part.at[s, core], line_in.at[slot], line_ss.at[slot], line_rs.at[slot], at((g + rel) % LINE, h, z)
         )
 
-    def steer_rows(s_ref, xs, ys, put):
-        def steer(i, carry):
-            rows = pl.ds(pl.multiple_of(i * 16, 16), 16)
+    def steer(start, count, spec, cs):
+        s_ref, turns = spec
+        xs = turns[0:1, :]
+        ys = turns[1:2, :]
+        for t in range(0, count, 16):
+            rows = pl.ds(pl.multiple_of(start + t, 16), 16)
             s0 = s_ref[0, rows, :]
             s1 = s_ref[1, rows, :]
             s0 = jnp.concatenate([s0] * 4, axis=1)
             s1 = jnp.concatenate([s1] * 4, axis=1)
             c, s = cos_sin(s0 * xs + s1 * ys)
-            put(rows, c.astype(jnp.bfloat16), s.astype(jnp.bfloat16))
-            return carry
-
-        lax.fori_loop(0, 32, steer, 0, unroll=4)
-
-    def a_step(s, carry):
-        k = s % 4
-        b = (s // 4) * 4 + (x + y + 1 + k) % LINE
-        freq = freq_ref[b]
-
-        def put(rows, c, s_):
-            cs_a[rows, 0:512] = c
-            cs_a[rows, 512:1024] = s_
-
-        steer_rows(sa, fraction(freq, place_a[0:1, :]), fraction(freq, place_a[1:2, :]), put)
+            cs[rows, 0:512] = c.astype(jnp.bfloat16)
+            cs[rows, 512:1024] = s.astype(jnp.bfloat16)
+
+    def a_bin(s):
+        return (s // 4) * 4 + (x + y + 1 + s % 4) % LINE
+
+    def a_spec(s, turns):
+        turns[...] = fraction(freq_ref[a_bin(s)], place_a[...])
+        return sa, turns
+
+    def b_spec(r, turns):
+        rows = [coord_in.at[0], coord_in.at[1], coord_in.at[2], place_b]
+        turns[...] = fraction(freq_ref[r * 4 + g], jnp.concatenate([q[...] for q in rows], axis=1))
+        return sb, turns
+
+    def a_dots(s, cs, spec, cs_next):
+        b = a_bin(s)
         cr = corr_v[0, b]
         ci = corr_v[1, b]
         rhs[0:512, 0:128] = cr
         rhs[0:512, 128:256] = ci
         rhs[512:1024, 0:128] = -ci
         rhs[512:1024, 128:256] = cr
-        w = jnp.dot(cs_a[...], rhs[...], preferred_element_type=jnp.float32)
+
+        w = jnp.dot(cs[...], rhs[...], preferred_element_type=jnp.float32)
         part[s, 0] = w[0:256]
         part[s, 1] = w[256:512]
-        core_copy(s).start()
-
-        @pl.when(s > 0)
-        def _():
-            finish(s - 1)
-
-        return carry
+        steer(0, 512, spec, cs_next)
 
     def finish(s):
         core_copy(s).wait_recv()
@@ -190,64 +189,58 @@
 
         @pl.when(rel > 0)
         def _():
-            line_copy(s, (s // 4) * 3 + rel - 1, rel).start()
-
-    def b_steer(r):
-        rows = [coord_in.at[0], coord_in.at[1], coord_in.at[2], place_b]
-        freq = freq_ref[r * 4 + g]
-        xs = fraction(freq, jnp.concatenate([q[0:1, :] for q in rows], axis=1))
-        ys = fraction(freq, jnp.concatenate([q[1:2, :] for q in rows], axis=1))
-
-        def put(rows, c, s):
-            for k in range(4):
-                cs_b[rows, k * 256 : k * 256 + 128] = c[:, k * 128 : k * 128 + 128]
-                cs_b[rows, k * 256 + 128 : k * 256 + 256] = s[:, k * 128 : k * 128 + 128]
-
-        steer_rows(sb, xs, ys, put)
-
-    def pair(half):
-        return (near, wrap) if half == 0 else (wrap, near)
-
-    def y1_copy(u, j):
-        first, _ = pair(u % 2)
+            slot = (s // 4) * 3 + rel - 1
+
+            line_copy(s, slot, rel).start()
+
+    def pair(d):
+        return (near, wrap) if d == 0 else (wrap, near)
+
+    def y1_copy(u, d, j):
+        first, _ = pair(d)
         block = diagonal if j == 0 else first
-        return remote(
-            y_part.at[u, block], y_in1.at[u, j], y1_ss.at[u * 2 + j], y1_rs.at[u * 2 + j], at(g, first, z)
-        )
-
-    def y2_copy(u):
-        _, second = pair(u % 2)
-        return remote(y_fwd.at[u], y_in2.at[u], y2_ss.at[u], y2_rs.at[u], at(g, second, z))
-
-    def b_side(r):
-        b_steer(r)
+        i = (u * 2 + d) * 2 + j
+        return remote(y_part.at[u, d, block], y_in1.at[u, d, j], y1_ss.at[i], y1_rs.at[i], at(g, first, z))
+
+    def y2_copy(u, d):
+        _, second = pair(d)
+        return remote(y_fwd.at[u, d], y_in2.at[u, d], y2_ss.at[u * 2 + d], y2_rs.at[u * 2 + d], at(g, second, z))
+
+    def b_side(r, cs, spec, cs_next):
         for k in range(4):
             if k < 3:
                 line_copy(0, r * 3 + k, k + 1).wait_recv()
             w = line_in[r * 3 + k] if k < 3 else part[r * 4 + 3 - h, core]
             hi = w.astype(jnp.bfloat16)
             lo = (w - hi.astype(jnp.float32)).astype(jnp.bfloat16)
+            re, im = slice(k * 128, k * 128 + 128), slice(512 + k * 128, 512 + k * 128 + 128)
             for dst, val in ((v_hi, hi), (v_lo, lo)):
-                dst[0:256, k * 256 : k * 256 + 256] = val
-                dst[256:512, k * 256 : k * 256 + 128] = val[:, 128:256]
-                dst[256:512, k * 256 + 128 : k * 256 + 256] = -val[:, 0:128]
+                dst[0:256, re] = val[:, 0:128]
+                dst[0:256, im] = val[:, 128:256]
+                dst[256:512, re] = val[:, 128:256]
+                dst[256:512, im] = -val[:, 0:128]
 
         dims = (((1,), (1,)), ((), ()))
+        for d in range(2):
+            part_d = slice(d * 256, d * 256 + 256)
+            v = lax.dot_general(cs[...], v_hi[part_d, :], dims, preferred_element_type=jnp.float32)
+            v = v + lax.dot_general(cs[...], v_lo[part_d, :], dims, preferred_element_type=jnp.float32)
+            for half in range(2):
+                for i in range(4):
+                    y_part[r * 2 + half, d, i] = v[half * 256 + i * 64 : half * 256 + i * 64 + 64]
+        if spec is not None:
+            steer(0, 512, spec, cs_next)
         for half in range(2):
-            u = r * 2 + half
-            steer = cs_b[half * 256 : half * 256 + 256, :]
-            v = lax.dot_general(steer, v_hi[...], dims, preferred_element_type=jnp.float32)
-            v = v + lax.dot_general(steer, v_lo[...], dims, preferred_element_type=jnp.float32)
-            for i in range(4):
-                y_part[u, i] = v[i * 64 : i * 64 + 64]
-            for j in range(2):
-                y1_copy(u, j).start()
+            for d in range(2):
+                for j in range(2):
+                    y1_copy(r * 2 + half, d, j).start()
 
     def y_forward(u):
-        _, second = pair(u % 2)
-        y1_copy(u, 0).wait_recv()
-        y_fwd[u] = y_part[u, second] + y_in1[u, 0]
-        y2_copy(u).start()
+        for d in range(2):
+            _, second = pair(d)
+            y1_copy(u, d, 0).wait_recv()
+            y_fwd[u, d] = y_part[u, d, second] + y_in1[u, d, 0]
+            y2_copy(u, d).start()
 
     def z_copy(u, k):
         return remote(
@@ -255,14 +248,15 @@
         )
 
     def z_send(u):
-        y1_copy(u, 1).wait_recv()
-        y2_copy(u).wait_recv()
-        t = y_part[u, h] + y_in1[u, 1] + y_in2[u]
+        t = []
+        for d in range(2):
+            y1_copy(u, d, 1).wait_recv()
+            y2_copy(u, d).wait_recv()
+            t.append(y_part[u, d, h] + y_in1[u, d, 1] + y_in2[u, d])
         for zh in range(4):
             for zl in range(2):
-                piece = t[zl * 32 : zl * 32 + 32]
                 z_out[u, zh * 2 + zl] = jnp.concatenate(
-                    [piece[:, zh * 64 : zh * 64 + 64], piece[:, 256 + zh * 64 : 256 + zh * 64 + 64]], axis=1
+                    [q[zl * 32 : zl * 32 + 32, zh * 64 : zh * 64 + 64] for q in t], axis=1
                 )
         for k in (3, 2, 4, 1, 5, 0, 6):
             z_copy(u, k).start()
@@ -287,30 +281,62 @@
             f_copy(u, k).start()
         out_ref[(u // 2) * 4 + g, (u % 2) * 8 : (u % 2) * 8 + 8, :] = f_out[u, g][:, 0:64]
 
-    def each(fn, *units):
-        for u in units:
-            fn(u)
-
-    loads[0].wait()
-    lax.fori_loop(0, 4, a_step, 0)
-    loads[1].wait()
-    lax.fori_loop(4, 8, a_step, 0)
-    for k in range(3):
-        coord_copy(k).wait_recv()
-    b_side(0)
-    loads[2].wait()
-    lax.fori_loop(8, 12, a_step, 0)
+    def steer_alone(spec, cs):
+        def some(i, carry):
+            steer(i * 64, 64, spec, cs)
+            return carry
+
+        lax.fori_loop(0, 8, some, 0)
+
+    steer_alone(a_spec(0, turns_0), cs_0)
+
+    def a_pair(i, carry):
+        s = i * 2
+
+        @pl.when(i % 2 == 0)
+        def _():
+            load(i // 2).wait()
+
+        a_dots(s, cs_0, a_spec(s + 1, turns_1), cs_1)
+
+        @pl.when(i == 0)
+        def _():
+            pl.semaphore_wait(barrier, len(peers))
+            for k in range(3):
+                coord_copy(k).start()
+
+        core_copy(s).start()
+
+        @pl.when(i > 0)
+        def _():
+            finish(s - 1)
+
+        a_dots(s + 1, cs_1, a_spec(jnp.minimum(s + 2, F - 1), turns_0), cs_0)
+        core_copy(s + 1).start()
+
+        finish(s)
+
+        @pl.when(i == 3)
+        def _():
+            for k in range(3):
+                coord_copy(k).wait_recv()
+            steer_alone(b_spec(0, turns_2), cs_2)
+            b_side(0, cs_2, b_spec(1, turns_3), cs_3)
+
+        return carry
+
+    lax.fori_loop(0, F // 2, a_pair, 0)
     finish(11)
     each(y_forward, 0, 1)
-    b_side(1)
+    b_side(1, cs_3, b_spec(2, turns_2), cs_2)
     each(z_send, 0, 1)
     each(y_forward, 2, 3)
-    b_side(2)
+    b_side(2, cs_2, None, None)
     each(z_send, 2, 3)
     each(power, 0, 1)
     each(y_forward, 4, 5)
+    each(z_send, 4, 5)
     each(power, 2, 3)
-    each(z_send, 4, 5)
     each(power, 4, 5)
     for u in range(UNITS):
         for k in range(3):
@@ -324,12 +350,13 @@
     lax.fori_loop(0, F, drain_core, 0)
     for k in range(3):
         coord_copy(k).wait_send()
-    for slot in range(9):
-        line_copy(0, slot, slot % 3 + 1).wait_send()
+    for k in range(9):
+        line_copy(0, k, k % 3 + 1).wait_send()
     for u in range(UNITS):
-        for j in range(2):
-            y1_copy(u, j).wait_send()
-        y2_copy(u).wait_send()
+        for d in range(2):
+            for j in range(2):
+                y1_copy(u, d, j).wait_send()
+            y2_copy(u, d).wait_send()
         for k in range(7):
             z_copy(u, k).wait_send()
         for k in range(3):
@@ -355,17 +382,23 @@
             pltpu.VMEM((2, 512, 128), i32),
             pltpu.VMEM((1024, 256), bf16),
             pltpu.VMEM((512, 1024), bf16),
+            pltpu.VMEM((512, 1024), bf16),
+            pltpu.VMEM((512, 1024), bf16),
+            pltpu.VMEM((512, 1024), bf16),
+            pltpu.VMEM((8, 512), i32),
+            pltpu.VMEM((8, 512), i32),
+            pltpu.VMEM((8, 512), i32),
+            pltpu.VMEM((8, 512), i32),
             pltpu.VMEM((F, 2, 256, 256), f32),
             pltpu.VMEM((F, 256, 256), f32),
             pltpu.VMEM((9, 256, 256), f32),
             pltpu.VMEM((3, 8, 128), i32),
             pltpu.VMEM((512, 1024), bf16),
             pltpu.VMEM((512, 1024), bf16),
-            pltpu.VMEM((512, 1024), bf16),
-            pltpu.VMEM((UNITS, LINE, 64, 512), f32),
-            pltpu.VMEM((UNITS, 2, 64, 512), f32),
-            pltpu.VMEM((UNITS, 64, 512), f32),
-            pltpu.VMEM((UNITS, 64, 512), f32),
+            pltpu.VMEM((UNITS, 2, LINE, 64, 256), f32),
+            pltpu.VMEM((UNITS, 2, 2, 64, 256), f32),
+            pltpu.VMEM((UNITS, 2, 64, 256), f32),
+            pltpu.VMEM((UNITS, 2, 64, 256), f32),
             pltpu.VMEM((UNITS, NZ, 32, 128), f32),
             pltpu.VMEM((UNITS * 7, 32, 128), f32),
             pltpu.VMEM((UNITS, LINE, 8, 128), f32),
@@ -374,8 +407,8 @@
             dma((F,)), dma((F,)),
             dma((9,)), dma((9,)),
             dma((3,)), dma((3,)),
-            dma((12,)), dma((12,)),
-            dma((UNITS,)), dma((UNITS,)),
+            dma((UNITS * 4,)), dma((UNITS * 4,)),
+            dma((UNITS * 2,)), dma((UNITS * 2,)),
             dma((UNITS * 7,)), dma((UNITS * 7,)),
             dma((UNITS * 3,)), dma((UNITS * 3,)),
         ],

time: 70.2 us -> 68.7 us (0.979); the launches traced: 69.3 us -> 68.6 us
  Pallas kernels: 67.8 us -> 67 us
    pallas_call x1, Pallas kernels: 67.8 us -> 67 us  [body(): pl.pallas_call(kernel, out_shape=jax.ShapeDtypeStruct((F, 16, 64), f32),...]
where the time goes in v3:
time: 68.7 us; the launch traced here: 68.6 us
  Pallas kernels  67 us (98%)
  local copies, waits for them, and re-layouts  1.54 us (2%)
    pallas_call x1, Pallas kernels, body(): pl.pallas_call(kernel, out_shape=jax.ShapeDtypeStruct((F, 16, 64), f32),...  67 us
    unnamed x1, local copies, waits for them, and re-layouts  1.54 us

profile of v3, /device:TPU:32, one launch (start us, length us, event | category | flops | bytes accessed | tf_op | source)
XLA Modules:
  0.0 68.6 jit_solution(8720842489248517292)
XLA Ops:
  0.0 67.0 %shard_map.82 = f32[12,16,64]{2,1,0:T(8,128)} custom-call(bf16[2,12,512,128]{3,2,1,0:T(8,128)(2,1)} %corr_hbm.1, s32[12]{0:T(128)} %freq_ref.1, s32[2,4096]{1,0:T(2,128)} %coords_a_ref.1, s32[2,4096]{1,0:T(2,128)} %coords_b_ref.1, s32[1,512]{1,0:T(1,128)} %bitcast.2, s32[1,128]{1,0:T(1,128)} %bitcast.3, s32[2,512]{1,0:T(2,128)} %slow_a_ref.1, ...), custom_call_target="tpu_custom_call" | custom-call | flops 7000000000 | bytes 4000000 | tf_op jit(solution)/shard_map/pallas_call | solution.py:370
  67.0 1.5 %copy.10 = f32[12,16,64]{2,1,0:T(8,128)} copy(f32[12,16,64]{2,1,0:T(8,128)} %shard_map.82) | data formatting | bytes 98304

commit v4 on v3

--- a/solution.py
+++ b/solution.py
@@ -65,7 +65,7 @@
            corr_v, grid_a, grid_b, place_a, place_b, sa, sb, rhs, cs_0, cs_1, cs_2, cs_3, turns_0, turns_1, turns_2, turns_3, part, core_in, line_in, coord_in,
            v_hi, v_lo, y_part, y_in1, y_fwd, y_in2, z_out, z_in, f_out, f_in,
            corr_sem, core_ss, core_rs, line_ss, line_rs, coord_ss, coord_rs,
-           y1_ss, y1_rs, y2_ss, y2_rs, z_ss, z_rs, f_ss, f_rs):
+           y1_ss, y1_rs, y2_ss, y2_rs, z_ss, z_rs, f_ss, f_rs, z_known):
     arow = lax.axis_index("arow")
     bcol = lax.axis_index("bcol")
     core = arow % 2
@@ -99,7 +99,7 @@
         load(r).start()
 
     barrier = pltpu.get_barrier_semaphore()
-    peers = [sibling, at(g, near, z), at(g, wrap, z)] + line_peer + z_peer
+    peers = [sibling, at(g, near, z), at(g, wrap, z)] + line_peer + [z_peer[0], z_peer[6]]
     for p in peers:
         pl.semaphore_signal(barrier, inc=1, device_id=p, device_id_type=MESH)
 
@@ -235,6 +235,14 @@
                 for j in range(2):
                     y1_copy(r * 2 + half, d, j).start()
 
+    def z_tell(n):
+        for d in range(2):
+            pl.semaphore_signal(z_known.at[n * 2 + d], inc=1, device_id=z_peer[6 * d], device_id_type=MESH)
+
+    def z_hear(n):
+        for d in range(2):
+            pl.semaphore_wait(z_known.at[n * 2 + d], 1)
+
     def y_forward(u):
         for d in range(2):
             _, second = pair(d)
@@ -302,6 +310,7 @@
         @pl.when(i == 0)
         def _():
             pl.semaphore_wait(barrier, len(peers))
+            z_tell(0)
             for k in range(3):
                 coord_copy(k).start()
 
@@ -318,6 +327,8 @@
 
         @pl.when(i == 3)
         def _():
+            z_hear(0)
+            z_tell(1)
             for k in range(3):
                 coord_copy(k).wait_recv()
             steer_alone(b_spec(0, turns_2), cs_2)
@@ -326,9 +337,12 @@
         return carry
 
     lax.fori_loop(0, F // 2, a_pair, 0)
+    z_hear(1)
+    z_tell(2)
     finish(11)
     each(y_forward, 0, 1)
     b_side(1, cs_3, b_spec(2, turns_2), cs_2)
+    z_hear(2)
     each(z_send, 0, 1)
     each(y_forward, 2, 3)
     b_side(2, cs_2, None, None)
@@ -411,6 +425,7 @@
             dma((UNITS * 2,)), dma((UNITS * 2,)),
             dma((UNITS * 7,)), dma((UNITS * 7,)),
             dma((UNITS * 3,)), dma((UNITS * 3,)),
+            pltpu.SemaphoreType.REGULAR((6,)),
         ],
         compiler_params=pltpu.CompilerParams(
             collective_id=0, has_side_effects=True, vmem_limit_bytes=56 * 2**20

time: 68.7 us -> 69 us (level)
  no operation moved by 1% of the time
where the time goes in v4:
time: 69 us; the launch traced here: 68.8 us
  Pallas kernels  67.2 us (97%)
  local copies, waits for them, and re-layouts  1.54 us (2%)
    pallas_call x1, Pallas kernels, body(): pl.pallas_call(kernel, out_shape=jax.ShapeDtypeStruct((F, 16, 64), f32),...  67.2 us
    unnamed x1, local copies, waits for them, and re-layouts  1.54 us

profile of v4, /device:TPU:32, one launch (start us, length us, event | category | flops | bytes accessed | tf_op | source)
XLA Modules:
  0.0 68.8 jit_solution(10897933234368985204)
XLA Ops:
  0.0 67.2 %shard_map.82 = f32[12,16,64]{2,1,0:T(8,128)} custom-call(bf16[2,12,512,128]{3,2,1,0:T(8,128)(2,1)} %corr_hbm.1, s32[12]{0:T(128)} %freq_ref.1, s32[2,4096]{1,0:T(2,128)} %coords_a_ref.1, s32[2,4096]{1,0:T(2,128)} %coords_b_ref.1, s32[1,512]{1,0:T(1,128)} %bitcast.2, s32[1,128]{1,0:T(1,128)} %bitcast.3, s32[2,512]{1,0:T(2,128)} %slow_a_ref.1, ...), custom_call_target="tpu_custom_call" | custom-call | flops 7000000000 | bytes 4000000 | tf_op jit(solution)/shard_map/pallas_call | solution.py:384
  67.2 1.5 %copy.10 = f32[12,16,64]{2,1,0:T(8,128)} copy(f32[12,16,64]{2,1,0:T(8,128)} %shard_map.82) | data formatting | bytes 98304
